TPU v7x, 128 devices: a whole 4x4x4 slice. The times are simulated.
128 devices in a mesh: pts: 8 (over x, core), cam: 16 (over z, y).
Axes of the slice: x: 4, y: 4, z: 4, core: 2. Of those that a mesh axis runs over, the one named last changes fastest.
Arguments:
- cam_params: float32 [9, 40960], P(None, 'cam')
- points: float32 [3, 262144], P(None, ('pts', 'cam'))
- measured: float32 [2, 8, 262144], P(None, None, ('pts', 'cam')), may hold values from -2 to 2
- obs_slot: int32 [8, 262144], P(None, ('pts', 'cam')), may hold values from 0 to 6143
- vis_tiles: int32 [128, 48], replicated, may hold values from 0 to 319, as said below
Outputs:
- camera_step: float32 [9, 40960], P(None, 'cam')
- point_step: float32 [3, 262144], P(None, ('pts', 'cam'))
Inputs may be any that keep to these rules, and one draw needn't show every extreme that they name: `vis_tiles`: each row is increasing and holds exactly 3 tiles of each block of 20 consecutive tiles.
All inputs are finite; a program needn't handle non-finite values.
Results may differ from a plain program's by a relative error of at most 0.0003.
Values sent between devices are 32-bit elements; how exact they have to be, the bound alone decides.
A program may use at most 64 MiB of HBM per device.

v0:
```python
import functools

import jax
import jax.numpy as jnp
from jax import lax
from jax.experimental import pallas as pl
from jax.experimental.pallas import tpu as pltpu
from jax.sharding import PartitionSpec as P

MESH = pl.DeviceIdType.MESH
F32 = jnp.float32
BF16 = jnp.bfloat16
DAMPING = 0.5

NP, NC = 8, 16
ND = NP * NC
VIEWS = 8
PB = 256
NB = 8
STEP = 4
OB = VIEWS * PB
TILES = 20
KP = 24
ROWS = 9
HI = 24
SL = ROWS * HI
PIECE = 16
SCAL = 48
PHASES = 7


def hop(step):
    return min(step, 4 - step)


OFFSETS = sorted(
    [(x, k, z, y) for x in range(4) for k in range(2) for z in range(4) for y in range(4) if x or k or z or y],
    key=lambda o: -(hop(o[0]) + hop(o[2]) + hop(o[3]) + 0.3 * o[1]),
)
PLANE = [o for o in OFFSETS if not (o[0] or o[1])]
COLUMN = [o for o in OFFSETS if not (o[2] or o[3])]


def neighbours():
    pts, cam = lax.axis_index("pts"), lax.axis_index("cam")
    x, k = lax.div(pts, 2), lax.rem(pts, 2)
    z, y = lax.div(cam, 4), lax.rem(cam, 4)
    xs = [lax.rem(x + d, 4) * 2 for d in range(4)]
    ks = [k, 1 - k]
    zs = [lax.rem(z + d, 4) * 4 for d in range(4)]
    ys = [lax.rem(y + d, 4) for d in range(4)]
    columns = {(dx, dk): xs[dx] + ks[dk] for dx in range(4) for dk in range(2)}
    planes = {(dz, dy): zs[dz] + ys[dy] for dz in range(4) for dy in range(4)}
    return lambda o: (columns[o[0], o[1]], planes[o[2], o[3]])


def message(ref, index, rows):
    return ref.at[pl.ds(pl.multiple_of(index * rows, rows), rows), :]


def dot(a, b):
    return jnp.dot(a, b, preferred_element_type=F32)


def dot_nt(a, b):
    return lax.dot_general(a, b, (((1,), (1,)), ((), ())), preferred_element_type=F32)


def split(x, parts):
    out = []
    for _ in range(parts - 1):
        top = x.astype(BF16)
        out.append(top)
        x = x - top.astype(F32)
    out.append(x.astype(BF16))
    return out


def iota(shape, dim):
    return lax.broadcasted_iota(jnp.int32, shape, dim)


def total(x):
    return jnp.sum(jnp.sum(x, axis=0, keepdims=True), axis=1, keepdims=True)


def lanes(x, shift):
    shift = shift % 128
    return x if shift == 0 else pltpu.roll(x, shift, 1)


def cross(a, b):
    return (a[1] * b[2] - a[2] * b[1], a[2] * b[0] - a[0] * b[2], a[0] * b[1] - a[1] * b[0])


def dot3(a, b):
    return a[0] * b[0] + a[1] * b[1] + a[2] * b[2]


def jacobians(cam, point):
    w, t = cam[0:3], cam[3:6]
    focal, k1, k2 = cam[6:9]
    across = cross(w, point)
    twice = cross(w, across)
    turn = tuple(across[i] + twice[i] for i in range(3))
    factor = 2.0 / (1.0 + dot3(w, w))
    moved = tuple(point[i] + factor * turn[i] + t[i] for i in range(3))
    inv = 1.0 / moved[2]
    q = (moved[0] * inv, moved[1] * inv)
    s = q[0] * q[0] + q[1] * q[1]
    gain = 1.0 + k1 * s + k2 * s * s
    slope = 2.0 * focal * (k1 + 2.0 * k2 * s)
    base = focal * gain
    value = (base * q[0], base * q[1])
    mixed = slope * q[0] * q[1]
    rows = ((base + slope * q[0] * q[0], mixed), (mixed, base + slope * q[1] * q[1]))
    jac_cam, jac_pnt = [], []
    for i in range(2):
        v0, v1 = rows[i][0] * inv, rows[i][1] * inv
        v = (v0, v1, -(v0 * q[0] + v1 * q[1]))
        m = cross(v, w)
        mm = cross(m, w)
        jac_pnt.append([v[n] + factor * (m[n] + mm[n]) for n in range(3)])
        first = cross(point, tuple(v[n] + m[n] for n in range(3)))
        second = cross(across, v)
        shrink = factor * dot3(v, turn)
        rot = [factor * (first[n] + second[n] - shrink * w[n]) for n in range(3)]
        fs = focal * s * q[i]
        jac_cam.append(rot + list(v) + [gain * q[i], fs, fs * s])
    return jac_cam, jac_pnt, value


def inverse3(jac_pnt):
    n = [[None] * 3 for _ in range(3)]
    for a in range(3):
        for b in range(a, 3):
            whole = jnp.sum(jac_pnt[0][a] * jac_pnt[0][b] + jac_pnt[1][a] * jac_pnt[1][b], axis=0, keepdims=True)
            n[a][b] = n[b][a] = whole + DAMPING if a == b else whole
    c00 = n[1][1] * n[2][2] - n[1][2] * n[2][1]
    c01 = n[1][2] * n[2][0] - n[1][0] * n[2][2]
    c02 = n[1][0] * n[2][1] - n[1][1] * n[2][0]
    c11 = n[0][0] * n[2][2] - n[0][2] * n[2][0]
    c12 = n[0][1] * n[2][0] - n[0][0] * n[2][1]
    c22 = n[0][0] * n[1][1] - n[0][1] * n[1][0]
    r = 1.0 / (n[0][0] * c00 + n[0][1] * c01 + n[0][2] * c02)
    return [c00 * r, c01 * r, c02 * r, c11 * r, c12 * r, c22 * r]


def apply_inverse(inv, v):
    return (
        inv[0] * v[0] + inv[1] * v[1] + inv[2] * v[2],
        inv[1] * v[0] + inv[3] * v[1] + inv[4] * v[2],
        inv[2] * v[0] + inv[4] * v[1] + inv[5] * v[2],
    )


def kernel(
    vis_h, cam_h, pts_h, meas_h, slot_h,
    cam_out, pnt_out,
    vis_s, vis_v, cam_ref, pts_ref, meas_ref, slot_ref,
    camt, src0, dst0, src, dst, fsrc, fdst, srcx, dstx,
    hot, hid_ref, t_ref, jc_ref, jp_ref, inv_ref, grad_ref, w_ref, terms_ref,
    gath, cols, acc, acc2, z_ref, d_ref, sel, selt, s1o, d2o, p0_ref, p2_ref, uq,
    insems, sem0, sends, recvs, fsem, semx, ready,
):
    pts, cam = lax.axis_index("pts"), lax.axis_index("cam")
    me = pts * NC + cam
    there = neighbours()

    barrier = pltpu.get_barrier_semaphore()
    for offset in PLANE + COLUMN:
        pl.semaphore_signal(barrier, inc=1, device_id=there(offset), device_id_type=MESH)

    pairs = ((vis_h, vis_s), (cam_h, cam_ref), (slot_h, slot_ref), (vis_h, vis_v), (pts_h, pts_ref), (meas_h, meas_ref))
    loads = [pltpu.make_async_copy(a, b, insems.at[i]) for i, (a, b) in enumerate(pairs)]
    for load in loads:
        load.start()

    loads[0].wait()
    loads[1].wait()
    for k in range(TILES):
        camt[k, 0:9, :] = cam_ref[:, k * 128 : (k + 1) * 128]
    for c in range(NC):
        for j in range(3):
            one = camt[jnp.clip(vis_s[3 * cam + j, pts * NC + c] - TILES * cam, 0, TILES - 1)]
            src0[c * 32 + j * 8 : c * 32 + j * 8 + 8, :] = one[0:8]
            src0[c * 32 + 24 + j : c * 32 + 25 + j, :] = one[8:9]

    def build(b, _):
        slot = slot_ref[:, pl.ds(pl.multiple_of(b * PB, PB), PB)]
        place = slot // 128
        shard = (place * 171) // 512
        own = place - 3 * shard
        half = shard // 8
        hid_ref[b] = own * 8 + shard - 8 * half
        low = half * 128 + slot - 128 * place
        for v in range(VIEWS):
            row = jnp.broadcast_to(low[v : v + 1, :], (256, PB))
            hot[b, :, v * PB : (v + 1) * PB] = (row == iota((256, PB), 0)).astype(F32).astype(BF16)
        return 0

    loads[2].wait()
    lax.fori_loop(0, NB, build, 0)
    for load in loads[3:]:
        load.wait()

    spread_rows = []
    for t in range(3):
        row = (vis_v[pl.ds(3 * cam + t, 1), :] - TILES * cam).astype(F32)
        row = jnp.broadcast_to(row, (8, 128)).astype(BF16)
        put = ((iota((128, 512), 1) // 4) == iota((128, 512), 0)).astype(F32).astype(BF16)
        spread_rows.append(dot(row, put)[0:1, :])
    quarter = iota((1, 512), 1) % 4
    index = jnp.where(quarter == 0, spread_rows[0], jnp.where(quarter == 1, spread_rows[1], spread_rows[2]))
    index = jnp.where(quarter == 3, -1.0, index)
    tile_no = iota((KP, 512), 0).astype(F32)
    blocks = [(jnp.broadcast_to(index, (KP, 512)) == tile_no).astype(F32)]
    for t in range(3):
        this = jnp.where(quarter == 3, spread_rows[t], -1.0)
        blocks.append((jnp.broadcast_to(this, (KP, 512)) == tile_no).astype(F32))
    blocks.append(jnp.zeros((128 - 4 * KP, 512), F32))
    pick = jnp.concatenate(blocks, axis=0)
    sel[...] = pick.astype(BF16)
    selt[...] = pick.T.astype(BF16)

    pl.semaphore_wait(barrier, len(PLANE) + len(COLUMN))
    for offset in PLANE:
        _, c = there(offset)
        pltpu.make_async_remote_copy(
            message(src0, c, 32), message(dst0, cam, 32), sem0.at[0], sem0.at[1],
            device_id=(pts, c), device_id_type=MESH,
        ).start()
    for offset in COLUMN:
        pl.semaphore_signal(ready, inc=1, device_id=there(offset), device_id_type=MESH)
    pltpu.make_async_copy(message(src0, cam, 32), message(dst0, cam, 32), sem0.at[1]).start()
    pltpu.make_async_copy(src0, dst0, sem0.at[1]).wait()
    pl.semaphore_wait(ready, len(COLUMN))

    def send(phase):
        for offset in OFFSETS:
            p, c = there(offset)
            to = p * NC + c
            pltpu.make_async_remote_copy(
                message(src.at[phase], to, 4), message(dst.at[phase], me, 4), sends.at[phase], recvs.at[phase],
                device_id=(p, c), device_id_type=MESH,
            ).start()
        pltpu.make_async_copy(message(src.at[phase], me, 4), message(dst.at[phase], me, 4), recvs.at[phase]).start()

    def arrived(phase):
        pltpu.make_async_copy(src.at[phase], dst.at[phase], recvs.at[phase]).wait()

    def sent(phase):
        rows = pl.ds(0, 4 * ND - 4)
        pltpu.make_async_copy(src.at[phase, rows], dst.at[phase, rows], sends.at[phase]).wait()

    lane = iota((1, 128), 1)

    def send_collect(phase, from_ref):
        for r in range(8):
            for j in range(3):
                for half in range(2):
                    src[phase, pl.ds(r * 64 + half * 32 + j, 8, stride=4), :] = from_ref[
                        r * HI + j * 8 : r * HI + j * 8 + 8, half * 128 : half * 128 + 128
                    ]
        for half in range(2):
            last = [
                from_ref[8 * HI + j * 8 : 8 * HI + j * 8 + 8, half * 128 : half * 128 + 128] for j in range(3)
            ]
            for p in range(NP):
                row = jnp.zeros((8, 128), F32)
                for j in range(3):
                    row = jnp.where(lane // PIECE == j, lanes(last[j], PIECE * (j - p)), row)
                src[phase, pl.ds(p * 64 + half * 32 + 3, 8, stride=4), :] = row
        send(phase)

    def recv_collect(phase):
        arrived(phase)
        got = sum(dot(sel[...], part) for part in split(dst[phase], 3))
        row8 = sum(lanes(got[KP * (t + 1) : KP * (t + 2)], -PIECE * t) for t in range(3))
        row8 = jnp.where(lane < PIECE, row8, 0.0)
        return jnp.concatenate([got[0:KP], row8], axis=0)

    def send_deliver(phase, own, dots):
        rows = [own[0:KP]] + [lanes(own[KP:], PIECE * t) for t in range(3)]
        rows.append(jnp.zeros((128 - 4 * KP, 128), F32))
        stacked = jnp.concatenate(rows, axis=0)
        out = sum(dot(selt[...], part) for part in split(stacked, 3))
        note = jnp.zeros((1, 128), F32)
        for i, value in enumerate(dots):
            note = jnp.where(lane == SCAL + i, value, note)
        out = out + jnp.where(iota((512, 128), 0) % 4 == 3, note, 0.0)
        src[phase] = out
        send(phase)

    def recv_deliver(phase, to_ref):
        arrived(phase)
        notes = jnp.zeros((8, 128), F32)
        for half in range(2):
            for r in range(8):
                for j in range(3):
                    to_ref[r * HI + j * 8 : r * HI + j * 8 + 8, half * 128 : half * 128 + 128] = dst[
                        phase, pl.ds(r * 64 + half * 32 + j, 8, stride=4), :
                    ]
            last = [jnp.zeros((8, 128), F32)] * 3
            for p in range(NP):
                row = dst[phase, pl.ds(p * 64 + half * 32 + 3, 8, stride=4), :]
                notes = notes + row
                for j in range(3):
                    last[j] = jnp.where(lane // PIECE == p, lanes(row, PIECE * (p - j)), last[j])
            for j in range(3):
                to_ref[8 * HI + j * 8 : 8 * HI + j * 8 + 8, half * 128 : half * 128 + 128] = last[j]
        notes = jnp.sum(notes, axis=0, keepdims=True)
        return [jnp.sum(jnp.where(lane == SCAL + i, notes, 0.0), axis=1, keepdims=True) for i in range(4)]

    def load_columns(x, parts):
        for i, part in enumerate(split(x, parts)):
            cols[i] = part

    def gather(b, k, parts):
        hid = hid_ref[b]
        for v in range(VIEWS):
            column = hot[b, :, v * PB : (v + 1) * PB]
            found = sum(dot(cols[i], column) for i in range(parts))
            mask = jnp.broadcast_to(hid[v : v + 1, :], (HI, PB)) == iota((HI, PB), 0)
            for r in range(ROWS):
                piece = found[r * HI : (r + 1) * HI]
                gath[k, r, v : v + 1, :] = jnp.sum(jnp.where(mask, piece, 0.0), axis=0, keepdims=True)

    def scatter(b, k, terms, to_ref):
        hid = hid_ref[b]
        count = len(terms)
        for r in range(count):
            top = terms[r].astype(BF16).astype(F32)
            terms_ref[k, r] = top
            terms_ref[k, count + r] = terms[r] - top
        for v in range(VIEWS):
            mask = jnp.broadcast_to(hid[v : v + 1, :], (HI, PB)) == iota((HI, PB), 0)
            for r in range(2 * count):
                row = jnp.broadcast_to(terms_ref[k, r, v : v + 1, :], (HI, PB))
                t_ref[k, r * HI : (r + 1) * HI, v * PB : (v + 1) * PB] = jnp.where(mask, row, 0.0).astype(BF16)
        both = dot_nt(t_ref[k, 0 : 2 * count * HI], hot[b])
        to_ref[0 : count * HI] += both[0 : count * HI] + both[count * HI :]

    for half in range(2):
        for j in range(3):
            for r in range(8):
                d_ref[r * HI + j * 8 : r * HI + j * 8 + 8, half * 128 : half * 128 + 128] = dst0[
                    pl.ds(half * 256 + j * 8 + r, 8, stride=32), :
                ]
            d_ref[8 * HI + j * 8 : 8 * HI + j * 8 + 8, half * 128 : half * 128 + 128] = dst0[
                pl.ds(half * 256 + 24 + j, 8, stride=32), :
            ]
    load_columns(d_ref[...], 3)
    acc[...] = jnp.zeros_like(acc)

    def linearize(b, k):
        at = pl.ds(pl.multiple_of(b * PB, PB), PB)
        cams = [gath[k, r] for r in range(ROWS)]
        point = tuple(jnp.broadcast_to(pts_ref[i : i + 1, at], (VIEWS, PB)) for i in range(3))
        jac_cam, jac_pnt, value = jacobians(cams, point)
        residual = [value[i] - meas_ref[i, :, at] for i in range(2)]
        inv = inverse3(jac_pnt)
        grad = [
            -jnp.sum(jac_pnt[0][n] * residual[0] + jac_pnt[1][n] * residual[1], axis=0, keepdims=True)
            for n in range(3)
        ]
        moved = apply_inverse(inv, grad)
        for i in range(2):
            for r in range(ROWS):
                jc_ref[b, i * ROWS + r] = jac_cam[i][r]
            for n in range(3):
                jp_ref[b, i * 3 + n] = jac_pnt[i][n]
        for n in range(6):
            inv_ref[b, n : n + 1, :] = inv[n]
        for n in range(3):
            grad_ref[b, n : n + 1, :] = grad[n]
        left = [-residual[i] - dot3(jac_pnt[i], moved) for i in range(2)]
        squares = [jac_cam[0][r] * jac_cam[0][r] + jac_cam[1][r] * jac_cam[1][r] for r in range(ROWS)]
        scatter(b, k, squares + [jac_cam[0][r] * left[0] + jac_cam[1][r] * left[1] for r in range(ROWS)], acc)

    def linearize_group(group, _):
        for k in range(STEP):
            gather(STEP * group + k, k, 3)
        for k in range(STEP):
            linearize(STEP * group + k, k)
        return 0

    lax.fori_loop(0, NB // STEP, linearize_group, 0)
    send_collect(0, acc.at[0:SL])
    send_collect(1, acc.at[SL : 2 * SL])
    precond = recv_collect(0) + DAMPING
    remain = recv_collect(1)
    scaled = remain / precond
    direction = scaled
    send_deliver(2, scaled, [total(remain * scaled)])

    norm = recv_deliver(2, z_ref)[0]
    d_ref[...] = z_ref[...]

    def image_of(b, k, step):
        jac = [[jc_ref[b, i * ROWS + r] for r in range(ROWS)] for i in range(2)]
        jac_pnt = [[jp_ref[b, i * 3 + n] for n in range(3)] for i in range(2)]
        u = []
        for i in range(2):
            value = jac[i][0] * gath[k, 0]
            for r in range(1, ROWS):
                value = value + jac[i][r] * gath[k, r]
            u.append(value)
        w = [jnp.sum(jac_pnt[0][n] * u[0] + jac_pnt[1][n] * u[1], axis=0, keepdims=True) for n in range(3)]
        moved = apply_inverse([inv_ref[b, n : n + 1, :] for n in range(6)], w)
        left = [u[i] - dot3(jac_pnt[i], moved) for i in range(2)]
        return jac, u, w, moved, left

    def apply(group, step):
        for k in range(STEP):
            gather(STEP * group + k, k, 2)
        for k in range(STEP):
            b = STEP * group + k
            jac, _, w, _, left = image_of(b, k, step)
            for n in range(3):
                w_ref[step, b, n : n + 1, :] = w[n]
            scatter(b, k, [jac[0][r] * left[0] + jac[1][r] * left[1] for r in range(ROWS)], acc)
        return 0

    solved = None
    alphas = []
    for step in range(2):
        load_columns(d_ref[...], 2)
        acc[0:SL] = jnp.zeros((SL, 256), F32)
        lax.fori_loop(0, NB // STEP, lambda group, _: apply(group, step), 0)
        send_collect(3 + 2 * step, acc.at[0:SL])
        image = recv_collect(3 + 2 * step) + DAMPING * direction
        quot = image / precond
        send_deliver(
            4 + 2 * step, quot,
            [total(remain * scaled), total(direction * image), total(scaled * image), total(quot * image)],
        )
        rz, dim, zim, imq = recv_deliver(4 + 2 * step, acc2)
        alpha = rz / dim
        beta = (rz - 2.0 * alpha * zim + alpha * alpha * imq) / rz
        z_ref[...] = z_ref[...] - alpha * acc2[...]
        d_ref[...] = z_ref[...] + beta * d_ref[...]
        solved = alpha * direction if step == 0 else solved + alpha * direction
        remain = remain - alpha * image
        scaled = remain / precond
        direction = scaled + beta * direction
        alphas.append(alpha)

    srcx[0:KP] = solved[0:KP]
    srcx[KP : 2 * KP] = direction[0:KP]
    srcx[2 * KP :] = solved[KP:] + lanes(direction[KP:], PIECE)
    for offset in COLUMN:
        p, _ = there(offset)
        pltpu.make_async_remote_copy(
            srcx, message(dstx, pts, 3 * KP), semx.at[0], semx.at[1], device_id=(p, cam), device_id_type=MESH
        ).start()
    pltpu.make_async_copy(srcx, message(dstx, pts, 3 * KP), semx.at[1]).start()
    load_columns(d_ref[...], 2)
    uq[...] = jnp.zeros_like(uq)

    def finish(b, k):
        _, u, _, moved, left = image_of(b, k, 2)
        uq[...] += u[0] * left[0] + u[1] * left[1]
        rest = []
        for n in range(3):
            value = grad_ref[b, n : n + 1, :]
            for step in range(2):
                value = value - alphas[step] * w_ref[step, b, n : n + 1, :]
            rest.append(value)
        rest = apply_inverse([inv_ref[b, n : n + 1, :] for n in range(6)], rest)
        at = pl.ds(pl.multiple_of(b * PB, PB), PB)
        for n in range(3):
            p0_ref[n : n + 1, at] = rest[n]
            p2_ref[n : n + 1, at] = moved[n]

    def finish_group(group, _):
        for k in range(STEP):
            gather(STEP * group + k, k, 2)
        for k in range(STEP):
            finish(STEP * group + k, k)
        return 0

    lax.fori_loop(0, NB // STEP, finish_group, 0)
    mine = total(uq[...]) + DAMPING * total(direction * direction)
    norm = total(remain * scaled)
    fsrc[...] = jnp.where(lane == 0, mine, jnp.where(lane == 1, norm, 0.0)).reshape(1, 1, 128)
    for offset in OFFSETS:
        p, c = there(offset)
        pltpu.make_async_remote_copy(
            fsrc.at[0], fdst.at[me], fsem.at[0], fsem.at[1], device_id=(p, c), device_id_type=MESH
        ).start()
    fdst[me] = fsrc[0]

    pltpu.make_async_copy(dstx, dstx, semx.at[1]).wait()
    for part, out in ((0, s1o), (1, d2o)):
        tail = jnp.zeros((KP, 128), F32)
        for p in range(NP):
            tail = jnp.where(lane // PIECE == p, lanes(dstx[p * 3 * KP + 2 * KP : (p + 1) * 3 * KP], PIECE * (p - part)), tail)
        for k in range(TILES):
            out[0:8, k * 128 : (k + 1) * 128] = dstx[pl.ds(part * KP + k, 8, stride=3 * KP), :]
            out[8:9, k * 128 : (k + 1) * 128] = tail[k : k + 1]

    pltpu.make_async_copy(fdst.at[pl.ds(0, ND - 1)], fdst.at[pl.ds(0, ND - 1)], fsem.at[1]).wait()
    sums = jnp.sum(fdst[...], axis=0)
    dim = jnp.sum(jnp.where(lane == 0, sums, 0.0), axis=1, keepdims=True)
    rz = jnp.sum(jnp.where(lane == 1, sums, 0.0), axis=1, keepdims=True)
    alpha = rz / dim
    cam_out[...] = s1o[...] + alpha * d2o[...]
    pnt_out[...] = p0_ref[...] - alpha * p2_ref[...]

    pltpu.make_async_copy(src0.at[pl.ds(0, 480)], dst0.at[pl.ds(0, 480)], sem0.at[0]).wait()
    for phase in range(PHASES):
        sent(phase)
    rest = pl.ds(0, 7 * 3 * KP)
    pltpu.make_async_copy(dstx.at[rest], dstx.at[rest], semx.at[0]).wait()
    pltpu.make_async_copy(fdst.at[pl.ds(0, ND - 1)], fdst.at[pl.ds(0, ND - 1)], fsem.at[0]).wait()


def shards(cam_params, points, measured, obs_slot, vis_tiles):
    vmem = pl.BlockSpec(memory_space=pltpu.VMEM)
    dma = pltpu.SemaphoreType.DMA
    return pl.pallas_call(
        kernel,
        out_shape=(
            jax.ShapeDtypeStruct(cam_params.shape, F32),
            jax.ShapeDtypeStruct(points.shape, F32),
        ),
        in_specs=[pl.BlockSpec(memory_space=pl.ANY)] * 5,
        out_specs=(vmem, vmem),
        scratch_shapes=[
            pltpu.SMEM(vis_tiles.shape[::-1], jnp.int32),
            pltpu.VMEM(vis_tiles.shape[::-1], jnp.int32),
            pltpu.VMEM(cam_params.shape, F32),
            pltpu.VMEM(points.shape, F32),
            pltpu.VMEM(measured.shape, F32),
            pltpu.VMEM(obs_slot.shape, jnp.int32),
            pltpu.VMEM((TILES, 16, 128), F32),
            pltpu.VMEM((NC * 32, 128), F32),
            pltpu.VMEM((NC * 32, 128), F32),
            pltpu.VMEM((PHASES, ND * 4, 128), F32),
            pltpu.VMEM((PHASES, ND * 4, 128), F32),
            pltpu.VMEM((1, 1, 128), F32),
            pltpu.VMEM((ND, 1, 128), F32),
            pltpu.VMEM((3 * KP, 128), F32),
            pltpu.VMEM((NP * 3 * KP, 128), F32),
            pltpu.VMEM((NB, 256, OB), BF16),
            pltpu.VMEM((NB, VIEWS, PB), jnp.int32),
            pltpu.VMEM((STEP, 4 * SL, OB), BF16),
            pltpu.VMEM((NB, 2 * ROWS, VIEWS, PB), F32),
            pltpu.VMEM((NB, 6, VIEWS, PB), F32),
            pltpu.VMEM((NB, 8, PB), F32),
            pltpu.VMEM((NB, 8, PB), F32),
            pltpu.VMEM((2, NB, 8, PB), F32),
            pltpu.VMEM((STEP, 4 * ROWS, VIEWS, PB), F32),
            pltpu.VMEM((STEP, ROWS, VIEWS, PB), F32),
            pltpu.VMEM((3, SL, 256), BF16),
            pltpu.VMEM((2 * SL, 256), F32),
            pltpu.VMEM((SL, 256), F32),
            pltpu.VMEM((SL, 256), F32),
            pltpu.VMEM((SL, 256), F32),
            pltpu.VMEM((128, 512), BF16),
            pltpu.VMEM((512, 128), BF16),
            pltpu.VMEM((ROWS, TILES * 128), F32),
            pltpu.VMEM((ROWS, TILES * 128), F32),
            pltpu.VMEM((3, NB * PB), F32),
            pltpu.VMEM((3, NB * PB), F32),
            pltpu.VMEM((VIEWS, PB), F32),
            dma((6,)),
            dma((2,)),
            dma((PHASES,)),
            dma((PHASES,)),
            dma((2,)),
            dma((2,)),
            pltpu.SemaphoreType.REGULAR,
        ],
        compiler_params=pltpu.CompilerParams(
            collective_id=0, has_side_effects=True, vmem_limit_bytes=60 << 20
        ),
    )(vis_tiles.T, cam_params, points, measured, obs_slot)


def solution(mesh):
    placed = (
        P(None, "cam"),
        P(None, ("pts", "cam")),
        P(None, None, ("pts", "cam")),
        P(None, ("pts", "cam")),
        P(),
    )
    return jax.shard_map(
        shards,
        mesh=mesh,
        in_specs=placed,
        out_specs=(P(None, "cam"), P(None, ("pts", "cam"))),
        check_vma=False,
    )
```

profile of v0, /device:TPU:1, one launch (start us, length us, event | category | flops | bytes accessed | tf_op | source)
XLA Modules:
  0.0 105.6 jit_solution(12522385590793631117)
XLA Ops:
  0.6 102.7 %shard_map.68 = (f32[9,2560]{1,0:T(8,128)}, f32[3,2048]{1,0:T(4,128)}) custom-call(s32[48,128]{1,0:T(8,128)} %bitcast.1, f32[9,2560]{1,0:T(8,128)} %cam_h.1, f32[3,2048]{1,0:T(4,128)} %pts_h.1, f32[2,8,2048]{2,1,0:T(8,128)} %meas_h.1, s32[8,2048]{1,0:T(8,128)} %slot_h.1), custom_call_target="tpu_custom_call" | custom-call | tf_op jit(solution)/shard_map/pallas_call | solution.py:522
  103.3 0.0 copy-start
  103.3 1.6 %copy.9 = f32[9,2560]{1,0:T(8,128)} copy(f32[9,2560]{1,0:T(8,128)} %get-tuple-element.4) | data formatting | bytes 184320
  104.9 0.0 copy-done
  104.9 0.6 copy.10
Async XLA Ops:
  103.3 1.6 %copy-start = (f32[3,2048]{1,0:T(4,128)S(1)}, f32[3,2048]{1,0:T(4,128)}, u32[]{:S(2)}) copy-start(f32[3,2048]{1,0:T(4,128)} %get-tuple-element.5) | copy-start | bytes 73732
where the time goes:
time: 106 us
  Pallas kernels  103 us (97%)
  local copies, waits for them, and re-layouts  2.22 us (2%)
    pallas_call x1, Pallas kernels, shards(): pl.pallas_call(kernel, out_shape=(jax.ShapeDtypeStruct(cam_params.shape,...  103 us
    unnamed x4, local copies, waits for them, and re-layouts  2.22 us

commit v1 on v0

--- a/solution.py
+++ b/solution.py
@@ -335,9 +335,10 @@
             terms_ref[k, count + r] = terms[r] - top
         for v in range(VIEWS):
             mask = jnp.broadcast_to(hid[v : v + 1, :], (HI, PB)) == iota((HI, PB), 0)
-            for r in range(2 * count):
-                row = jnp.broadcast_to(terms_ref[k, r, v : v + 1, :], (HI, PB))
-                t_ref[k, r * HI : (r + 1) * HI, v * PB : (v + 1) * PB] = jnp.where(mask, row, 0.0).astype(BF16)
+            for r in range(0, 2 * count, 2):
+                rows = [jnp.broadcast_to(terms_ref[k, r + n, v : v + 1, :], (HI, PB)) for n in range(2)]
+                both = jnp.concatenate([jnp.where(mask, row, 0.0) for row in rows], axis=0)
+                t_ref[k, r * HI : (r + 2) * HI, v * PB : (v + 1) * PB] = both.astype(BF16)
         both = dot_nt(t_ref[k, 0 : 2 * count * HI], hot[b])
         to_ref[0 : count * HI] += both[0 : count * HI] + both[count * HI :]
 

time: 106 us -> 106 us (level)
  no operation moved by 1% of the time
where the time goes in v1:
time: 106 us
  Pallas kernels  103 us (97%)
  local copies, waits for them, and re-layouts  2.22 us (2%)
    pallas_call x1, Pallas kernels, shards(): pl.pallas_call(kernel, out_shape=(jax.ShapeDtypeStruct(cam_params.shape,...  103 us
    unnamed x4, local copies, waits for them, and re-layouts  2.22 us

profile of v1, /device:TPU:1, one launch (start us, length us, event | category | flops | bytes accessed | tf_op | source)
XLA Modules:
  0.0 105.6 jit_solution(3854460177479871866)
XLA Ops:
  0.6 102.7 %shard_map.68 = (f32[9,2560]{1,0:T(8,128)}, f32[3,2048]{1,0:T(4,128)}) custom-call(s32[48,128]{1,0:T(8,128)} %bitcast.1, f32[9,2560]{1,0:T(8,128)} %cam_h.1, f32[3,2048]{1,0:T(4,128)} %pts_h.1, f32[2,8,2048]{2,1,0:T(8,128)} %meas_h.1, s32[8,2048]{1,0:T(8,128)} %slot_h.1), custom_call_target="tpu_custom_call" | custom-call | tf_op jit(solution)/shard_map/pallas_call | solution.py:523
  103.4 0.0 copy-start
  103.4 1.6 %copy.9 = f32[9,2560]{1,0:T(8,128)} copy(f32[9,2560]{1,0:T(8,128)} %get-tuple-element.4) | data formatting | bytes 184320
  105.0 0.0 copy-done
  105.0 0.6 copy.10
Async XLA Ops:
  103.4 1.6 %copy-start = (f32[3,2048]{1,0:T(4,128)S(1)}, f32[3,2048]{1,0:T(4,128)}, u32[]{:S(2)}) copy-start(f32[3,2048]{1,0:T(4,128)} %get-tuple-element.5) | copy-start | bytes 73732
